TPU v7x, 256 devices: a whole 4x4x8 slice. The times are simulated.
256 devices in a mesh: seq: 32 (over z, x_hi, core), chan: 8 (over x_lo, y).
Axes of the slice: x: 4 (x_hi: 2, x_lo: 2; x = x_hi * 2 + x_lo), y: 4, z: 8, core: 2. Of those that a mesh axis runs over, the one named last changes fastest.
Arguments:
- features: bfloat16 [8192, 3, 8192], P('seq', None, 'chan'), may hold values from -6 to 6
- residual_in: bfloat16 [8192, 8192], P('seq', 'chan'), may hold values from -6 to 6
- short_filter: float32 [3, 3, 8192], P(None, None, 'chan'), may hold values from -3.5 to 3.5
- decay_rates: float32 [8192, 16], P('chan'), as said below
- residues: float32 [8192, 16], P('chan'), may hold values from -0.12 to 0.12
- skip_gain: float32 [8192], P('chan'), may hold values from -4 to 4
- out_weight: bfloat16 [8192, 8192], P('chan', 'seq'), may hold values from -0.125 to 0.125
- final_gain: float32 [8192], P('chan'), may hold values from 0.5 to 1.5
- embedding: bfloat16 [512, 8192], P(None, 'chan')
- next_ids: int32 [8192], P('seq'), may hold values from 65 to 84, as said below
Outputs:
- block_out: bfloat16 [8192, 8192], P('seq', 'chan')
- log_like: float32 [8192], P('seq')
Inputs may be any that keep to these rules, and one draw needn't show every extreme that they name: `next_ids`: each entry is one of 65, 67, 71, 84. `decay_rates`: all between 1.2e-5 and 0.05.
All inputs are finite; a program needn't handle non-finite values.
Results may differ from a plain program's by a relative error of at most 0.015.
Values may be sent and summed in bfloat16 or wider, within the bound.
A program may use at most 128 MiB of HBM per device.

v0:
```python
import jax
import jax.numpy as jnp
from jax import lax
from jax.sharding import PartitionSpec as P


def shifted(value, axis, steps):
    count = lax.axis_size(axis)
    first, last = (max(0, -steps), min(count, count - steps))
    return lax.ppermute(value, axis, [(source, source + steps) for source in range(first, last)])


def short_conv(padded, taps_weight, count):
    short_len = taps_weight.shape[0]
    output = taps_weight[0] * padded[short_len - 1 : short_len - 1 + count]
    for offset in range(1, short_len):
        output = (
            output
            + taps_weight[offset] * padded[short_len - 1 - offset : short_len - 1 - offset + count]
        )
    return output


def modal_conv(signal, rates_part, residue_part, start_state):
    channels, length = signal.shape
    block_len = min(128, length)
    blocks = length // block_len
    shaped = signal.reshape(channels, blocks, block_len)
    offsets = jnp.arange(block_len, dtype=jnp.float32)
    middle = 0.5 * (block_len - 1)
    falling = residue_part[:, :, None] * jnp.exp(
        -rates_part[:, :, None] * (offsets - middle)[None, None, :]
    )
    rising = jnp.exp(rates_part[:, :, None] * (offsets - middle)[None, None, :])
    full_lag = jnp.einsum("cma,cmb->cab", falling, rising, precision=lax.Precision.HIGHEST)
    positions = jnp.arange(block_len, dtype=jnp.int32)
    causal = positions[:, None] >= positions[None, :]
    toeplitz = jnp.where(causal[None], full_lag, 0.0)
    inside = jnp.einsum("cab,cnb->cna", toeplitz, shaped, precision=lax.Precision.HIGHEST)
    end_decay = jnp.exp(-rates_part[:, :, None] * (block_len - 1 - offsets)[None, None, :])
    states = jnp.einsum("cmb,cnb->cmn", end_decay, shaped, precision=lax.Precision.HIGHEST)
    target = jnp.arange(blocks + 1, dtype=jnp.int32)
    source = jnp.arange(blocks, dtype=jnp.int32)
    gap = (target[:, None] - 1 - source[None, :]).astype(jnp.float32)
    before = target[:, None] > source[None, :]
    span = rates_part * block_len
    weights = jnp.where(
        before[None, None],
        jnp.exp(-span[:, :, None, None] * jnp.maximum(gap, 0.0)[None, None]),
        0.0,
    )
    from_start = (
        jnp.exp(-span[:, :, None] * target.astype(jnp.float32)[None, None, :])
        * start_state[:, :, None]
    )
    entering = (
        jnp.einsum("cmnk,cmk->cmn", weights, states, precision=lax.Precision.HIGHEST) + from_start
    )
    previous = entering[:, :, :blocks]
    last_state = entering[:, :, blocks]
    mode_lift = residue_part[:, :, None] * jnp.exp(
        -rates_part[:, :, None] * (offsets + 1.0)[None, None, :]
    )
    carried = jnp.einsum("cma,cmn->cna", mode_lift, previous, precision=lax.Precision.HIGHEST)
    return ((inside + carried).reshape(channels, length), last_state)


def modal_grouped(signal, rates_part, residue_part, start_state):
    channels = signal.shape[0]
    group_size = min(128, channels)
    groups = channels // group_size

    def one_group(pieces):
        return modal_conv(pieces[0], pieces[1], pieces[2], pieces[3])

    outputs, states = lax.map(
        one_group,
        (
            signal.reshape(groups, group_size, -1),
            rates_part.reshape(groups, group_size, -1),
            residue_part.reshape(groups, group_size, -1),
            start_state.reshape(groups, group_size, -1),
        ),
    )
    return (outputs.reshape(channels, -1), states.reshape(channels, -1))


def local(
    features,
    residual_in,
    short_filter,
    decay_rates,
    residues,
    skip_gain,
    out_weight,
    final_gain,
    embedding,
    next_ids,
):
    tok_rows = features.shape[0]
    short_len = short_filter.shape[0]
    rim_rows = shifted(features[tok_rows - (short_len - 1) :], "seq", 1)
    padded = jnp.concatenate([rim_rows, features], axis=0).astype(jnp.float32)
    streams = short_conv(padded, short_filter, tok_rows)
    queries = streams[:, 0, :]
    mixed_kv = (streams[:, 1, :] * streams[:, 2, :]).astype(jnp.bfloat16)
    by_channel = lax.all_to_all(mixed_kv.T, "seq", split_axis=0, concat_axis=1, tiled=True)
    chan_count = by_channel.shape[0]
    chan_start = lax.axis_index("seq") * chan_count
    rates_part = lax.dynamic_slice_in_dim(decay_rates, chan_start, chan_count, 0)
    residue_part = lax.dynamic_slice_in_dim(residues, chan_start, chan_count, 0)
    convolved, unused_state = modal_grouped(
        by_channel.astype(jnp.float32),
        rates_part,
        residue_part,
        jnp.zeros((chan_count, decay_rates.shape[1]), jnp.float32),
    )
    returned = lax.all_to_all(
        convolved.astype(jnp.bfloat16), "seq", split_axis=1, concat_axis=0, tiled=True
    )
    filtered = returned.T
    gated = (
        queries * (filtered.astype(jnp.float32) + skip_gain * mixed_kv.astype(jnp.float32))
    ).astype(jnp.bfloat16)
    partial_out = jnp.dot(
        gated,
        lax.all_gather(out_weight, "seq", axis=1, tiled=True),
        preferred_element_type=jnp.float32,
    )
    summed = lax.psum_scatter(partial_out, "chan", scatter_dimension=1, tiled=True)
    block_out = (residual_in.astype(jnp.float32) + summed).astype(jnp.bfloat16)
    block_f = block_out.astype(jnp.float32)
    width_all = block_f.shape[1] * lax.axis_size("chan")
    scaled = (block_f * final_gain).astype(jnp.bfloat16)
    partial_logits = lax.dot_general(
        scaled, embedding, (((1,), (1,)), ((), ())), preferred_element_type=jnp.float32
    )
    sum_squares, raw_logits = (
        lax.psum(jnp.sum(block_f * block_f, axis=1).astype(jnp.bfloat16), "chan").astype(
            jnp.float32
        ),
        lax.psum(partial_logits.astype(jnp.bfloat16), "chan").astype(jnp.float32),
    )
    inv_rms = lax.rsqrt(sum_squares / width_all + 1e-06)
    logits = raw_logits * inv_rms[:, None]
    vocab_ids = jnp.arange(logits.shape[1], dtype=jnp.int32)
    one_hot = next_ids[:, None] == vocab_ids[None, :]
    chosen = jnp.sum(jnp.where(one_hot, logits, 0.0), axis=1)
    log_like = chosen - jax.nn.logsumexp(logits, axis=1)
    return (block_out, log_like)


def solution(mesh):
    return jax.shard_map(
        local,
        mesh=mesh,
        in_specs=(
            P("seq", None, "chan"),
            P("seq", "chan"),
            P(None, None, "chan"),
            P("chan", None),
            P("chan", None),
            P("chan"),
            P("chan", "seq"),
            P("chan"),
            P(None, "chan"),
            P("seq"),
        ),
        out_specs=(P("seq", "chan"), P("seq")),
        check_vma=False,
    )
```

profile of v0, /device:TPU:6, one launch (start us, length us, event | category | flops | bytes accessed | tf_op | source)
XLA Modules:
  0.0 375.3 jit_solution(12228247012403409512)
XLA Ops:
  7.2 0.7 all-gather.2.cloned.1.call-update
  7.9 0.8 slice.35
  8.7 1.9 collective-permute-start
  10.7 0.8 multiply_negate_fusion
  11.5 0.8 slice_bitcast_fusion.3
  12.3 1.7 copy.38
  14.3 1.0 collective-permute-done
  15.7 1.0 maximum_convert_fusion
  16.7 3.2 fusion.8
  19.8 1.6 copy-done.1
  21.5 0.9 fusion.20
  22.4 12.3 %all-to-all-start = ((bf16[32,32,256]{2,1,0:T(8,128)(2,1)}), bf16[32,32,256]{2,1,0:T(8,128)(2,1)}, u32[]{:S(2)}, u32[]{:S(2)}) async-start(bf16[32,32,256]{2,1,0:T(8,128)(2,1)} %bitcast.6), calls=%async_computation | async-start | bytes 1048576 | tf_op jit(solution)/shard_map/all_to_all | solution.py:107
  35.0 3.7 fusion.38
  38.6 17.6 %all-to-all-done = bf16[32,32,256]{2,1,0:T(8,128)(2,1)} async-done(((bf16[32,32,256]{2,1,0:T(8,128)(2,1)}), bf16[32,32,256]{2,1,0:T(8,128)(2,1)}, u32[]{:S(2)}, u32[]{:S(2)}) %all-to-all-start) | async-done | bytes 524320 | tf_op jit(solution)/shard_map/all_to_all | solution.py:107
  56.2 2.1 copy.39
  58.4 2.0 reshape.121
  60.4 2.0 fusion.35
  62.4 33.2 %fusion = f32[32,16,1,65]{3,2,1,0:T(1,128)S(1)} fusion(f32[32,16,64,1]{2,3,1,0:T(1,128)S(1)} %bitcast.40, f32[65,64]{0,1:T(8,128)S(1)} %convert_maximum_fusion, f32[32,16]{1,0:T(8,128)S(1)} %copy.43, pred[65,64]{0,1:T(8,128)(4,1)S(1)} %iota_compare_fusion.2), kind=kOutput, calls=%fused_computation | convolution fusion | flops 29818880 | bytes 287040 | tf_op jit(solution)/shard_map/while/body/eval_jaxpr/cmnk,cmk->cmn/dot_general | solution.py:57
  95.6 2.1 fusion.28
  97.7 3.0 fusion.15
  100.7 1.2 convert_element_type.82
  102.2 22.6 %all_to_all.26 = bf16[32,32,256]{2,0,1:T(8,128)(2,1)S(1)} all-to-all(bf16[32,32,256]{2,0,1:T(8,128)(2,1)S(1)} %copy.45), channel_id=1, replica_groups=mesh['seq'=32,'chan'=8] {'seq'}, dimensions={1} | all-to-all | bytes 1048576 | tf_op jit(solution)/shard_map/all_to_all | solution.py:118
  124.8 2.2 fusion.22
  127.0 52.3 %all-gather.2.cloned.1.call-done = bf16[1024,8192]{1,0:T(8,128)(2,1)} async-done(((bf16[1024,256]{1,0:T(8,128)(2,1)}), bf16[1024,8192]{1,0:T(8,128)(2,1)}) %all-gather.2.cloned.1.call-update) | async-done | bytes 16777232 | tf_op jit(solution)/shard_map/all_gather | solution.py:127
  179.3 12.7 %fusion.59 = f32[256,8192]{1,0:T(8,128)} fusion(bf16[256,1024]{0,1:T(8,128)(2,1)S(1)} %fusion.22, bf16[1024,8192]{1,0:T(8,128)(2,1)} %all-gather.2.cloned.1.call-done), kind=kOutput, calls=%fused_computation.87 | convolution fusion | flops 4294967296 | bytes 25690112 | tf_op jit(solution)/shard_map/dot_general | solution.py:125
  192.1 92.9 %reduce-scatter.2.cloned.1.call-done = f32[256,1024]{1,0:T(8,128)} async-done(((f32[256,8192]{1,0:T(8,128)}), f32[256,1024]{1,0:T(8,128)}) %reduce-scatter.2.cloned.1.call-update) | async-done | bytes 1048592 | tf_op jit(solution)/shard_map/reduce_scatter | solution.py:130
  285.0 1.5 fusion.19
  286.5 1.2 convolution_convert_fusion
  287.7 17.1 %psum.15 = bf16[256]{0:T(256)(128)(2,1)S(1)} all-reduce(bf16[256]{0:T(256)(128)(2,1)S(1)} %get-tuple-element.14), channel_id=1, replica_groups=mesh['seq'=32,'chan'=8] {'chan'}, use_global_device_ids=true, to_apply=%region_3.4 | all-reduce | flops 256 | bytes 1024 | tf_op jit(solution)/shard_map/psum | solution.py:139
  304.8 60.9 %all-reduce.2.cloned.1.call-done = bf16[256,512]{1,0:T(8,128)(2,1)} async-done(((bf16[256,512]{1,0:T(8,128)(2,1)}), bf16[256,512]{1,0:T(8,128)(2,1)}) %all-reduce.2.cloned.1.call-update) | async-done | bytes 262160 | tf_op jit(solution)/shard_map/psum | solution.py:142
  365.7 1.1 fusion.26
  366.9 1.3 exponential_reduce_fusion
  (38 shorter events, 2.1 us)
Async XLA Ops:
  7.2 279.3 %copy-start = (bf16[512,1024]{1,0:T(8,128)(2,1)S(1)}, bf16[512,1024]{1,0:T(8,128)(2,1)}, u32[]{:S(2)}) copy-start(bf16[512,1024]{1,0:T(8,128)(2,1)} %param.18) | copy-start | bytes 3145732
  7.2 172.2 %all-gather.2.cloned.1.call-start = ((), (), s32[]{:S(2)}) async-start(), calls=%async_computation.3 | async-start | bytes 17301504 | tf_op jit(solution)/shard_map/all_gather | solution.py:127
  8.7 6.5 %collective-permute-start = (bf16[2,3,1024]{2,0,1:T(2,128)(2,1)S(1)}, bf16[2,3,1024]{2,0,1:T(2,128)(2,1)S(1)}, u32[]{:S(2)}, u32[]{:S(2)}) collective-permute-start(bf16[2,3,1024]{2,0,1:T(2,128)(2,1)S(1)} %slice.35), channel_id=1, source_target_pairs={{0,8},{8,16},{16,24},{24,32},{32,40},{40,48},{48,56},{56,64},{64,7... | collective-permute-start | bytes 36872 | tf_op jit(solution)/shard_map/ppermute | solution.py:10
  19.8 1.6 copy-start.1
  22.4 33.8 %all-to-all-start = ((bf16[32,32,256]{2,1,0:T(8,128)(2,1)}), bf16[32,32,256]{2,1,0:T(8,128)(2,1)}, u32[]{:S(2)}, u32[]{:S(2)}) async-start(bf16[32,32,256]{2,1,0:T(8,128)(2,1)} %bitcast.6), calls=%async_computation | async-start | bytes 1048576 | tf_op jit(solution)/shard_map/all_to_all | solution.py:107
  34.6 250.4 %reduce-scatter.2.cloned.1.call-start = ((), (), s32[]{:S(2)}) async-start(), calls=%async_computation.4 | async-start | bytes 9437184 | tf_op jit(solution)/shard_map/reduce_scatter | solution.py:130
  62.4 35.3 %copy-start.2 = (bf16[32,64,128]{2,1,0:T(8,128)(2,1)S(1)}, bf16[32,64,128]{2,1,0:T(8,128)(2,1)}, u32[]{:S(2)}) copy-start(bf16[32,64,128]{2,1,0:T(8,128)(2,1)} %reshape.121) | copy-start | bytes 1572868
  97.7 27.1 %copy-start.5 = (f32[1024]{0:T(1024)S(1)}, f32[1024]{0:T(1024)}, u32[]{:S(2)}) copy-start(f32[1024]{0:T(1024)} %param.15) | copy-start | bytes 12292
  192.0 93.0 %copy-start.3 = (bf16[256,1024]{1,0:T(8,128)(2,1)S(1)}, bf16[256,1024]{1,0:T(8,128)(2,1)}, u32[]{:S(2)}) copy-start(bf16[256,1024]{1,0:T(8,128)(2,1)} %param.11) | copy-start | bytes 1572868
  192.0 94.5 %copy-start.7 = (f32[1024]{0:T(1024)S(1)}, f32[1024]{0:T(1024)}, u32[]{:S(2)}) copy-start(f32[1024]{0:T(1024)} %param.17) | copy-start | bytes 12292
  192.1 174.8 %copy-start.6 = (s32[256]{0:T(256)S(1)}, s32[256]{0:T(256)}, u32[]{:S(2)}) copy-start(s32[256]{0:T(256)} %param.19) | copy-start | bytes 3076
  192.1 173.7 %all-reduce.2.cloned.1.call-start = ((), (), s32[]{:S(2)}) async-start(), calls=%async_computation.5 | async-start | bytes 524288 | tf_op jit(solution)/shard_map/psum | solution.py:142
  286.5 82.3 %copy-start.4 = (bf16[256,1024]{1,0:T(8,128)(2,1)}, bf16[256,1024]{1,0:T(8,128)(2,1)S(1)}, u32[]{:S(2)}) copy-start(bf16[256,1024]{1,0:T(8,128)(2,1)S(1)} %get-tuple-element.20) | copy-start | bytes 1572868
Sparse Core Ops, SparseCore 0:
  10.6 168.7 all-gather.1
  192.2 92.7 reduce-scatter.1
  287.8 77.8 all-reduce.1
where the time goes:
time: 376 us; the launch traced here: 375 us
  waiting for transfers between devices  225 us (60%)
  matrix products  57.8 us (15%)
  blocking collectives  39.7 us (11%)
  starting transfers between devices  14.5 us (4%)
  between operations  14 us (4%)
  other arithmetic  12.5 us (3%)
  local copies, waits for them, and re-layouts  11.3 us (3%)
    reduce_scatter x1, waiting for transfers between devices, local(): lax.psum_scatter(partial_out, 'chan', scatter_dimension=1, tiled=True)  92.9 us
    psum x1, waiting for transfers between devices, local(): lax.psum(partial_logits.astype(jnp.bfloat16), 'chan').astype(jnp.float32)  60.9 us
    all_gather x1, waiting for transfers between devices, local(): lax.all_gather(out_weight, 'seq', axis=1, tiled=True)  52.3 us
    dot_general x1, matrix products, modal_conv(): jnp.einsum('cmnk,cmk->cmn', weights, states, precision=lax.Precision.HIGH...  33.2 us
    all_to_all x1, blocking collectives, local(): lax.all_to_all(convolved.astype(jnp.bfloat16), 'seq', split_axis=1, conca...  22.6 us
    all_to_all x1, waiting for transfers between devices, local(): lax.all_to_all(mixed_kv.T, 'seq', split_axis=0, concat_axis=1, tiled=True)  17.6 us
    psum x1, blocking collectives, local(): lax.psum(jnp.sum(block_f * block_f, axis=1).astype(jnp.bfloat16), 'chan')  17.1 us
    dot_general x1, matrix products, local(): jnp.dot(gated, lax.all_gather(out_weight, 'seq', axis=1, tiled=True), pre...  12.7 us
  transfers between devices with their start and end apart: 5, of which 5 were waited for; matrix products, arithmetic and copies ran while one was open for 16% of the time, Pallas kernels for 0%

commit v1 on v0

v1 whole, which is shorter than its diff:
```python
import functools

import jax
import jax.numpy as jnp
from jax import lax
from jax.experimental import pallas as pl
from jax.experimental.pallas import tpu as pltpu
from jax.sharding import PartitionSpec as P


F32 = jnp.float32
BF16 = jnp.bfloat16
MESH = pl.DeviceIdType.MESH
GROUP = 4
HALO = 2
TAPS = 3
STREAMS = 3
SUB = 8
PAIR = 16


def kernel(
    Z,
    Y,
    x_hbm,
    res_hbm,
    taps_ref,
    rates_ref,
    resid_ref,
    skip_ref,
    w_hbm,
    gain_ref,
    emb_hbm,
    ids_ref,
    bo_hbm,
    ll_ref,
    x_v,
    xf,
    taps,
    rate,
    coef,
    dec1,
    dec_t,
    dec_g,
    halo,
    kv,
    qf,
    g0,
    st,
    p1,
    e_z,
    p2,
    p3_send,
    p3,
    w_all,
    a_all,
    c_send,
    c_recv,
    o_send,
    o_recv,
    res_v,
    emb_v,
    bo_v,
    l_send,
    l_recv,
    s_send,
    s_recv,
    loc_sem,
    halo_sem,
    p1_sem,
    p2_ssem,
    p2_rsem,
    p3_sem,
    sw_sem,
    w_ssem,
    w_rsem,
    sib_ssem,
    sib_rsem,
    a_ssem,
    a_rsem,
    c_ssem,
    c_rsem,
    o_ssem,
    o_rsem,
    l_sem,
    s_sem,
):
    T = x_hbm.shape[1]
    C = x_hbm.shape[2]
    LN = C // SUB
    modes = rates_ref.shape[0]
    MQ = modes // GROUP
    QR = MQ * SUB
    KH = w_hbm.shape[0] // 2
    NB = w_hbm.shape[1]
    SEQ = Z * GROUP
    CHAN = 2 * Y
    NX = 4
    VB = emb_hbm.shape[0] // CHAN
    HT = T // 2

    seq = lax.axis_index("seq")
    chan = lax.axis_index("chan")
    z = seq // 4
    g = seq % 4
    x_hi = g // 2
    core = g % 2
    x_lo = chan // Y
    y = chan % Y
    xx = 2 * x_hi + x_lo

    def dev(zz, gg, cc):
        return {"seq": zz * 4 + gg, "chan": cc}

    def x_dev(xn):
        return dev(z, (xn // 2) * 2 + core, (xn % 2) * Y + y)

    def rcopy(src, dst, ssem, rsem, target):
        return pltpu.make_async_remote_copy(
            src_ref=src, dst_ref=dst, send_sem=ssem, recv_sem=rsem, device_id=target, device_id_type=MESH
        )

    barrier = pltpu.get_barrier_semaphore()
    partners = [dev((z + d) % Z, g, chan) for d in range(1, Z)]
    partners += [dev(z, (g + r) % 4, chan) for r in range(1, 4)]
    partners += [{"seq": (seq + 1) % SEQ, "chan": chan}, {"seq": (seq + SEQ - 1) % SEQ, "chan": chan}]
    partners += [x_dev((xx + r) % NX) for r in range(1, NX)]
    partners += [dev(z, g, (chan + r) % CHAN) for r in range(1, CHAN)]
    swap = dev(z, x_hi * 2 + (1 - core), (1 - x_lo) * Y + y)
    partners += [swap]
    for partner in partners:
        pl.semaphore_signal(barrier, inc=1, device_id=partner, device_id_type=MESH)

    loads = [pltpu.make_async_copy(x_hbm.at[i], x_v.at[i], loc_sem.at[i]) for i in range(STREAMS)]
    load_res = pltpu.make_async_copy(res_hbm, res_v, loc_sem.at[3])
    load_emb = pltpu.make_async_copy(emb_hbm, emb_v, loc_sem.at[4])
    load_w = pltpu.make_async_copy(w_hbm, w_all.at[core, z], loc_sem.at[5])
    native = core == x_lo

    @pl.when(native)
    def _():
        load_w.start()

    for load in loads:
        load.start()
    load_res.start()
    load_emb.start()

    for j in range(SUB):
        lanes = slice(j * LN, (j + 1) * LN)
        rate[pl.ds(j, modes, stride=SUB), :] = rates_ref[:, lanes]
        coef[pl.ds(j, modes, stride=SUB), :] = resid_ref[:, lanes]
        for t in range(TAPS):
            for i in range(STREAMS):
                taps[(t * STREAMS + i) * SUB + j : (t * STREAMS + i) * SUB + j + 1, :] = taps_ref[t, i : i + 1, lanes]
    dec1[...] = jnp.exp(-rate[...])
    dec_t[...] = jnp.exp(-rate[...] * float(T))
    dec_g[...] = jnp.exp(-rate[...] * float(T * GROUP))

    for load in loads:
        load.wait()

    def spread(b):
        rows = pl.ds(pl.multiple_of(b * PAIR, PAIR), PAIR)
        for i in range(STREAMS):
            for j in range(SUB):
                block = x_v[i, rows, j * LN : (j + 1) * LN].astype(F32)
                xf[i, pl.ds(b * PAIR * SUB + j, PAIR, stride=SUB), :] = block

    spread(T // PAIR - 1)
    pl.semaphore_wait(barrier, len(partners))

    halo_copy = rcopy(
        xf.at[:, pl.ds((T - HALO) * SUB, HALO * SUB), :],
        halo,
        halo_sem.at[0],
        halo_sem.at[1],
        {"seq": (seq + 1) % SEQ, "chan": chan},
    )
    halo_copy.start()

    swap_copy = rcopy(w_hbm, w_all.at[x_lo, z], sw_sem.at[0], sw_sem.at[1], swap)

    @pl.when(jnp.logical_not(native))
    def _():
        swap_copy.start()

    up = dev((z + 1) % Z, g, chan)
    down = dev((z + Z - 1) % Z, g, chan)
    sibling = dev(z, x_hi * 2 + (1 - core), chan)
    HALF = Z // 2

    def w_chunk(k, zz, h):
        return w_all.at[k, zz, pl.ds(h * KH, KH), :]

    def ring_copy(flow, d, h):
        if flow == 0:
            zz, target, index = (z + Z - d + 1) % Z, up, 2 * d
        else:
            zz, target, index = (z + d - 1) % Z, down, 2 * d - 1
        if d == HALF:
            index = Z - 1
        ref = w_chunk(core, zz, h)
        return rcopy(ref, ref, w_ssem.at[flow, d - 1, h], w_rsem.at[index, h], target)

    def ring_halves(flow, d):
        return (0, 1) if d < HALF else ((0,) if flow == 0 else (1,))

    def rel(i):
        d = (i + 1) // 2
        return (z + Z + jnp.where(i % 2 == 1, d, -d)) % Z

    def sib_copy(i, h):
        ref = w_chunk(core, rel(i), h)
        return rcopy(ref, ref, sib_ssem.at[i, h], sib_rsem.at[i, h], sibling)

    @pl.when(native)
    def _():
        load_w.wait()

    @pl.when(jnp.logical_not(native))
    def _():
        rcopy(w_hbm, w_all.at[core, z], sw_sem.at[0], sw_sem.at[1], swap).wait_recv()

    for h in range(2):
        for flow in range(2):
            if HALF == 1 and h not in ring_halves(flow, 1):
                continue
            ring_copy(flow, 1, h).start()
    for h in range(2):
        sib_copy(0, h).start()

    def pump(d):
        for h in range(2):
            for flow in range(2):
                if h not in ring_halves(flow, d):
                    continue
                ring_copy(flow, d, h).wait_recv()
                if d < HALF and h in ring_halves(flow, d + 1):
                    ring_copy(flow, d + 1, h).start()
                i = Z - 1 if d == HALF else (2 * d if flow == 0 else 2 * d - 1)
                sib_copy(i, h).start()

    lax.fori_loop(0, T // PAIR - 1, lambda b, c: (spread(b), c)[1], 0)

    halo_copy.wait_recv()
    first = seq == 0

    def tap(t, i):
        return taps[(t * STREAMS + i) * SUB : (t * STREAMS + i + 1) * SUB, :]

    def halo_tile(i, n):
        return jnp.where(first, 0.0, halo[i, n * SUB : (n + 1) * SUB, :])

    def rows_of(t):
        return pl.ds(pl.multiple_of(t * SUB, SUB), SUB)

    def short(i, now, before, before2):
        return tap(0, i) * now + tap(1, i) * before + tap(2, i) * before2

    def mode(ref, m):
        return ref[m * SUB : (m + 1) * SUB, :]

    UN = 4
    zero = jnp.zeros((SUB, LN), F32)

    def state_step(n, carry):
        k1, k2, v1, v2, *s = carry
        for u in range(UN):
            rows = rows_of(n * UN + u)
            k0, v0 = xf[1, rows, :], xf[2, rows, :]
            value = short(1, k0, k1, k2) * short(2, v0, v1, v2)
            kv[rows, :] = value
            s = [mode(dec1, m) * s[m] + value for m in range(modes)]
            k1, k2, v1, v2 = k0, k1, v0, v1
        return (k1, k2, v1, v2, *s)

    last = lax.fori_loop(
        0,
        T // UN,
        state_step,
        (halo_tile(1, 1), halo_tile(1, 0), halo_tile(2, 1), halo_tile(2, 0)) + (zero,) * modes,
    )
    for m in range(modes):
        st[m * SUB : (m + 1) * SUB, :] = last[4 + m]

    def quarter(j):
        return pl.ds(pl.multiple_of(j * QR, QR), QR)

    def p1_copy(r):
        peer = (g + r) % 4
        return rcopy(st.at[quarter(peer), :], p1.at[g], p1_sem.at[0, r - 1], p1_sem.at[1, r - 1], dev(z, peer, chan))

    for r in range(1, 4):
        p1_copy(r).start()
    p1[g] = st[quarter(g), :]

    def local_step(n, carry):
        q1, q2, *s = carry
        for u in range(UN):
            rows = rows_of(n * UN + u)
            q0, value = xf[0, rows, :], kv[rows, :]
            s = [mode(dec1, m) * s[m] + value for m in range(modes)]
            terms = [mode(coef, m) * s[m] for m in range(modes)]
            while len(terms) > 1:
                terms = [terms[2 * n_] + terms[2 * n_ + 1] for n_ in range(len(terms) // 2)]
            qf[rows, :] = short(0, q0, q1, q2)
            g0[rows, :] = terms[0] + skip_ref[...] * value
            q1, q2 = q0, q1
        return (q1, q2, *s)

    for r in range(1, 4):
        p1_copy(r).wait_recv()
    my_t = dec_t[quarter(g), :]
    total = p1[0]
    for j in range(1, 4):
        total = total * my_t + p1[j]
    e_z[...] = total

    def p2_copy(zz, src_z):
        return rcopy(e_z, p2.at[src_z], p2_ssem.at[zz], p2_rsem.at[src_z], dev(zz, g, chan))

    lax.fori_loop(z + 1, Z, lambda zz, c: (p2_copy(zz, z).start(), c)[1], 0)

    lax.fori_loop(0, T // UN, local_step, (halo_tile(0, 1), halo_tile(0, 0)) + (zero,) * modes)

    my_g = dec_g[quarter(g), :]

    def carry_in(zz, c):
        p2_copy(zz, zz).wait_recv()
        return c * my_g + p2[zz]

    enter = lax.fori_loop(0, z, carry_in, jnp.zeros((QR, LN), F32))
    for j in range(4):
        p3_send[j] = enter
        enter = enter * my_t + p1[j]

    def p3_copy(r):
        peer = (g + r) % 4
        return rcopy(p3_send.at[peer], p3.at[quarter(g), :], p3_sem.at[0, r - 1], p3_sem.at[1, r - 1], dev(z, peer, chan))

    for r in range(1, 4):
        p3_copy(r).start()
    p3[quarter(g), :] = p3_send[g]
    pump(1)
    for r in range(1, 4):
        p3_copy(r).wait_recv()

    def gate_step(n, w):
        w = list(w)
        for u in range(UN):
            rows = rows_of(n * UN + u)
            w = [mode(dec1, m) * w[m] for m in range(modes)]
            terms = w
            while len(terms) > 1:
                terms = [terms[2 * n_] + terms[2 * n_ + 1] for n_ in range(len(terms) // 2)]
            g0[rows, :] = qf[rows, :] * (g0[rows, :] + terms[0])
        return tuple(w)

    lax.fori_loop(0, T // UN, gate_step, tuple(mode(coef, m) * mode(p3, m) for m in range(modes)))

    def gather_rows(b, c):
        rows = pl.ds(pl.multiple_of(b * PAIR, PAIR), PAIR)
        for j in range(SUB):
            block = g0[pl.ds(b * PAIR * SUB + j, PAIR, stride=SUB), :]
            a_all[xx, rows, j * LN : (j + 1) * LN] = block.astype(BF16)
        return c

    lax.fori_loop(0, T // PAIR, gather_rows, 0)

    right, left = (xx + 1) % NX, (xx + NX - 1) % NX

    def a_copy(way, block, h, slot):
        ref = a_all.at[block, pl.ds(h * HT, HT), :]
        return rcopy(ref, ref, a_ssem.at[slot, h], a_rsem.at[slot, h], x_dev(right if way == 0 else left))

    for h in range(2):
        a_copy(0, xx, h, 0).start()
        a_copy(1, xx, 1 - h, 1).start()

    pump(2)
    a_copy(0, left, 0, 0).wait_recv()
    a_copy(0, left, 0, 2).start()
    a_copy(1, right, 1, 1).wait_recv()
    a_copy(1, right, 1, 2).start()
    a_copy(0, left, 1, 0).wait_recv()
    a_copy(1, right, 0, 1).wait_recv()

    def c_copy(tb, zz):
        peer, half = zz % Y, zz // Y
        dy = (peer + Y - y) % Y
        return rcopy(
            c_send.at[tb, zz],
            c_recv.at[jnp.maximum(dy - 1, 0), tb, half],
            c_ssem.at[tb, zz],
            c_rsem.at[jnp.maximum(dy - 1, 0), tb, half],
            dev(z, g, x_lo * Y + peer),
        )

    def unit(tb, i):
        zz = rel(i)
        total = jnp.dot(a_all[2 * tb], w_all[0, zz], preferred_element_type=F32)
        total += jnp.dot(a_all[2 * tb + 1], w_all[1, zz], preferred_element_type=F32)
        c_send[tb, zz] = total.astype(BF16)

        @pl.when(zz % Y != y)
        def _():
            c_copy(tb, zz).start()

    def sib_wait(i):
        for h in range(2):
            ref = w_chunk(1 - core, rel(i), h)
            rcopy(ref, ref, sib_ssem.at[i, h], sib_rsem.at[i, h], sibling).wait_recv()

    NEAR = max(Z - 3, 1)

    def near_first(i, c):
        sib_wait(i)
        unit(x_hi, i)
        return c

    def near_second(i, c):
        unit(1 - x_hi, i)
        return c

    def both(i, c):
        sib_wait(i)
        unit(x_hi, i)
        unit(1 - x_hi, i)
        return c

    lax.fori_loop(0, NEAR, near_first, 0)
    for d in range(3, HALF):
        pump(d)
    a_copy(0, (xx + 2) % NX, 0, 2).wait_recv()
    a_copy(1, (xx + 2) % NX, 1, 2).wait_recv()
    lax.fori_loop(0, NEAR, near_second, 0)
    lax.fori_loop(NEAR, Z - 1, both, 0)
    if HALF > 2:
        pump(HALF)
    lax.fori_loop(Z - 1, Z, both, 0)

    def o_copy(tb, half):
        target = 2 * tb + half
        r = (target + NX - xx) % NX
        return rcopy(
            o_send.at[tb, half], o_recv.at[xx], o_ssem.at[tb, half], o_rsem.at[jnp.maximum(r - 1, 0)], x_dev(target)
        )

    def sum_step(n, c):
        tb = (x_hi + n // 2) % 2
        half = n % 2
        total = c_send[tb, half * Y + y].astype(F32)
        for dy in range(1, Y):
            src = c_recv.at[dy - 1, tb, half]
            rcopy(src, src, c_ssem.at[tb, half], c_rsem.at[dy - 1, tb, half], sibling).wait_recv()
            total += c_recv[dy - 1, tb, half].astype(F32)
        value = total.astype(BF16)
        mine = 2 * tb + half == xx

        @pl.when(mine)
        def _():
            o_recv[xx] = value

        @pl.when(jnp.logical_not(mine))
        def _():
            o_send[tb, half] = value
            o_copy(tb, half).start()

        return c

    lax.fori_loop(0, 4, sum_step, 0)
    load_res.wait()
    load_emb.wait()
    for r in range(1, NX):
        src = o_recv.at[(xx + NX - r) % NX]
        rcopy(src, src, o_ssem.at[0, 0], o_rsem.at[r - 1], sibling).wait_recv()

    squares = jnp.zeros((T, LN), F32)
    scaled = []
    for j in range(NX):
        cols = slice(j * NB, (j + 1) * NB)
        value = (res_v[:, cols].astype(F32) + o_recv[j].astype(F32)).astype(BF16)
        bo_v[:, cols] = value
        wide = value.astype(F32)
        for n in range(NB // LN):
            part = wide[:, n * LN : (n + 1) * LN]
            squares += part * part
        scaled.append((wide * gain_ref[:, cols]).astype(BF16))
    store_bo = pltpu.make_async_copy(bo_v, bo_hbm, loc_sem.at[6])
    store_bo.start()

    logits = jnp.zeros((VB * CHAN, T), F32)
    for j in range(NX):
        logits += lax.dot_general(
            emb_v[:, j * NB : (j + 1) * NB], scaled[j], (((1,), (1,)), ((), ())), preferred_element_type=F32
        )
    sums = jnp.sum(squares.T, axis=0, keepdims=True)
    high = sums.astype(BF16)
    low = (sums - high.astype(F32)).astype(BF16)
    row = lax.broadcasted_iota(jnp.int32, (PAIR, T), 0)
    extra = jnp.where(row == 0, high.astype(F32), jnp.where(row == 1, low.astype(F32), 0.0)).astype(BF16)
    for j in range(CHAN):
        l_send[j, :VB, :] = logits[j * VB : (j + 1) * VB, :].astype(BF16)
        l_send[j, VB:, :] = extra

    def l_copy(r):
        peer = (chan + r) % CHAN
        return rcopy(l_send.at[peer], l_recv.at[r - 1], l_sem.at[0, r - 1], l_sem.at[1, r - 1], dev(z, g, peer))

    for r in range(1, CHAN):
        l_copy(r).start()
    full = l_send[chan].astype(F32)
    for r in range(1, CHAN):
        l_copy(r).wait_recv()
        full += l_recv[r - 1].astype(F32)
    mean = (full[VB : VB + 1, :] + full[VB + 1 : VB + 2, :]) / float(C * CHAN)
    scaled_logits = full[:VB, :] * lax.rsqrt(mean + 1e-06)
    vocab = lax.broadcasted_iota(jnp.int32, (VB, T), 0) + chan * VB
    chosen = jnp.sum(jnp.where(vocab == ids_ref[...], scaled_logits, 0.0), axis=0, keepdims=True)
    top = jnp.max(scaled_logits, axis=0, keepdims=True)
    mass = jnp.sum(jnp.exp(scaled_logits - top), axis=0, keepdims=True)
    row = lax.broadcasted_iota(jnp.int32, (SUB, T), 0)
    s_send[...] = jnp.where(row == 0, top, jnp.where(row == 1, mass, jnp.where(row == 2, chosen, 0.0)))

    def s_copy(r):
        return rcopy(
            s_send, s_recv.at[r - 1], s_sem.at[0, r - 1], s_sem.at[1, r - 1], dev(z, g, (chan + r) % CHAN)
        )

    for r in range(1, CHAN):
        s_copy(r).start()
    best = top
    for r in range(1, CHAN):
        s_copy(r).wait_recv()
        best = jnp.maximum(best, s_recv[r - 1, 0:1, :])
    mass = mass * jnp.exp(top - best)
    for r in range(1, CHAN):
        mass += s_recv[r - 1, 1:2, :] * jnp.exp(s_recv[r - 1, 0:1, :] - best)
        chosen += s_recv[r - 1, 2:3, :]
    ll_ref[...] = chosen - best - jnp.log(mass)

    store_bo.wait()
    halo_copy.wait_send()

    @pl.when(jnp.logical_not(native))
    def _():
        swap_copy.wait_send()

    for flow in range(2):
        for d in range(1, HALF + 1):
            for h in ring_halves(flow, d):
                ring_copy(flow, d, h).wait_send()
    for i in range(Z):
        for h in range(2):
            sib_copy(i, h).wait_send()
    for r in range(1, 4):
        p1_copy(r).wait_send()
        p3_copy(r).wait_send()
    lax.fori_loop(z + 1, Z, lambda zz, c: (p2_copy(zz, z).wait_send(), c)[1], 0)
    for h in range(2):
        a_copy(0, xx, h, 0).wait_send()
        a_copy(1, xx, h, 1).wait_send()
    a_copy(0, left, 0, 2).wait_send()
    a_copy(1, right, 1, 2).wait_send()

    def c_done(n, c):
        tb, zz = n // Z, n % Z

        @pl.when(zz % Y != y)
        def _():
            c_copy(tb, zz).wait_send()

        return c

    lax.fori_loop(0, 2 * Z, c_done, 0)

    def o_done(n, c):
        @pl.when(n != xx)
        def _():
            o_copy(n // 2, n % 2).wait_send()

        return c

    lax.fori_loop(0, 4, o_done, 0)
    for r in range(1, CHAN):
        l_copy(r).wait_send()
        s_copy(r).wait_send()


def block(Z, Y, features, residual_in, short_filter, decay_rates, residues, skip_gain, out_weight, final_gain, embedding, next_ids):
    T, _, C = features.shape
    LN = C // SUB
    modes = decay_rates.shape[1]
    QR = modes // GROUP * SUB
    K, NB = out_weight.shape
    V = embedding.shape[0]
    CHAN = 2 * Y
    VB = V // CHAN
    DMA = pltpu.SemaphoreType.DMA
    hbm = pl.BlockSpec(memory_space=pl.ANY)
    vmem = pl.BlockSpec(memory_space=pltpu.VMEM)
    block_out, log_like = pl.pallas_call(
        functools.partial(kernel, Z, Y),
        out_shape=(jax.ShapeDtypeStruct((T, C), BF16), jax.ShapeDtypeStruct((1, T), F32)),
        in_specs=[hbm, hbm, vmem, vmem, vmem, vmem, hbm, vmem, hbm, vmem],
        out_specs=(hbm, vmem),
        scratch_shapes=[
            pltpu.VMEM((STREAMS, T, C), BF16),
            pltpu.VMEM((STREAMS, T * SUB, LN), F32),
            pltpu.VMEM((TAPS * STREAMS * SUB, LN), F32),
            pltpu.VMEM((modes * SUB, LN), F32),
            pltpu.VMEM((modes * SUB, LN), F32),
            pltpu.VMEM((modes * SUB, LN), F32),
            pltpu.VMEM((modes * SUB, LN), F32),
            pltpu.VMEM((modes * SUB, LN), F32),
            pltpu.VMEM((STREAMS, HALO * SUB, LN), F32),
            pltpu.VMEM((T * SUB, LN), F32),
            pltpu.VMEM((T * SUB, LN), F32),
            pltpu.VMEM((T * SUB, LN), F32),
            pltpu.VMEM((modes * SUB, LN), F32),
            pltpu.VMEM((GROUP, QR, LN), F32),
            pltpu.VMEM((QR, LN), F32),
            pltpu.VMEM((Z, QR, LN), F32),
            pltpu.VMEM((GROUP, QR, LN), F32),
            pltpu.VMEM((modes * SUB, LN), F32),
            pltpu.VMEM((2, Z, K, NB), BF16),
            pltpu.VMEM((4, T, C), BF16),
            pltpu.VMEM((2, Z, T, NB), BF16),
            pltpu.VMEM((Y - 1, 2, 2, T, NB), BF16),
            pltpu.VMEM((2, 2, T, NB), BF16),
            pltpu.VMEM((4, T, NB), BF16),
            pltpu.VMEM((T, C), BF16),
            pltpu.VMEM((V, C), BF16),
            pltpu.VMEM((T, C), BF16),
            pltpu.VMEM((CHAN, VB + PAIR, T), BF16),
            pltpu.VMEM((CHAN - 1, VB + PAIR, T), BF16),
            pltpu.VMEM((SUB, T), F32),
            pltpu.VMEM((CHAN - 1, SUB, T), F32),
            DMA((7,)),
            DMA((2,)),
            DMA((2, 3)),
            DMA((Z,)),
            DMA((Z,)),
            DMA((2, 3)),
            DMA((2,)),
            DMA((2, Z // 2, 2)),
            DMA((Z, 2)),
            DMA((Z, 2)),
            DMA((Z, 2)),
            DMA((3, 2)),
            DMA((3, 2)),
            DMA((2, Z)),
            DMA((Y - 1, 2, 2)),
            DMA((2, 2)),
            DMA((3,)),
            DMA((2, CHAN - 1)),
            DMA((2, CHAN - 1)),
        ],
        compiler_params=pltpu.CompilerParams(
            collective_id=0, has_side_effects=True, vmem_limit_bytes=60 * 1024 * 1024
        ),
    )(
        features.transpose(1, 0, 2),
        residual_in,
        short_filter,
        decay_rates.T,
        residues.T,
        skip_gain.reshape(SUB, LN),
        out_weight,
        final_gain.reshape(1, C),
        embedding,
        next_ids.reshape(1, T),
    )
    return block_out, log_like.reshape(T)


def solution(mesh):
    return jax.shard_map(
        functools.partial(block, mesh.shape["seq"] // 4, mesh.shape["chan"] // 2),
        mesh=mesh,
        in_specs=(
            P("seq", None, "chan"),
            P("seq", "chan"),
            P(None, None, "chan"),
            P("chan", None),
            P("chan", None),
            P("chan"),
            P("chan", "seq"),
            P("chan"),
            P(None, "chan"),
            P("seq"),
        ),
        out_specs=(P("seq", "chan"), P("seq")),
        check_vma=False,
    )
```

time: 376 us -> 99.5 us (0.26)
  waiting for transfers between devices: 225 us -> 0 us
  Pallas kernels: 0 us -> 95.6 us
  matrix products: 57.8 us -> 0 us
  blocking collectives: 39.7 us -> 0 us
  starting transfers between devices: 14.5 us -> 0 us
  between operations: 14 us -> 0.64 us
  other arithmetic: 12.5 us -> 0 us
  local copies, waits for them, and re-layouts: 11.3 us -> 3.07 us
    pallas_call x0 -> x1, Pallas kernels: none -> 95.6 us  [block(): pl.pallas_call(functools.partial(kernel, Z, Y), out_shape=(jax.ShapeDtype...]
    reduce_scatter x1 -> x0, waiting for transfers between devices: 92.9 us -> none  [local(): lax.psum_scatter(partial_out, 'chan', scatter_dimension=1, tiled=True)]
    psum x1 -> x0, waiting for transfers between devices: 60.9 us -> none  [local(): lax.psum(partial_logits.astype(jnp.bfloat16), 'chan').astype(jnp.float32)]
    dot_general x7 -> x0, matrix products: 57.8 us -> none  [the longest x1 33.2 us: modal_conv(): jnp.einsum('cmnk,cmk->cmn', weights, states, precision=lax.Precision.HIGH...]
    all_gather x1 -> x0, waiting for transfers between devices: 52.3 us -> none  [local(): lax.all_gather(out_weight, 'seq', axis=1, tiled=True)]
    all_to_all x1 -> x0, blocking collectives: 22.6 us -> none  [local(): lax.all_to_all(convolved.astype(jnp.bfloat16), 'seq', split_axis=1, conca...]
    all_to_all x1 -> x0, waiting for transfers between devices: 17.6 us -> none  [local(): lax.all_to_all(mixed_kv.T, 'seq', split_axis=0, concat_axis=1, tiled=True)]
    psum x1 -> x0, blocking collectives: 17.1 us -> none  [local(): lax.psum(jnp.sum(block_f * block_f, axis=1).astype(jnp.bfloat16), 'chan')]
  transfers between devices with their start and end apart: 5 -> 0, of which waited for: 5 -> 0; matrix products, arithmetic and copies ran while one was open for 16% -> 0% of each run, Pallas kernels for 0% -> 0%
where the time goes in v1:
time: 99.5 us; the launch traced here: 99.3 us
  Pallas kernels  95.6 us (96%)
  local copies, waits for them, and re-layouts  3.07 us (3%)
    pallas_call x1, Pallas kernels, block(): pl.pallas_call(functools.partial(kernel, Z, Y), out_shape=(jax.ShapeDtype...  95.6 us
    unnamed x2, local copies, waits for them, and re-layouts  3.07 us

profile of v1, /device:TPU:6, one launch (start us, length us, event | category | flops | bytes accessed | tf_op | source)
XLA Modules:
  0.0 99.3 jit_solution(14766570783907001735)
XLA Ops:
  0.6 95.6 %shard_map.113 = (bf16[256,1024]{1,0:T(8,128)(2,1)}, f32[1,256]{1,0:T(1,128)}) custom-call(bf16[3,256,1024]{2,1,0:T(8,128)(2,1)} %bitcast.7, bf16[256,1024]{1,0:T(8,128)(2,1)} %res_hbm.1, f32[3,3,1024]{2,1,0:T(4,128)} %taps_ref.1, f32[16,1024]{1,0:T(8,128)} %bitcast.8, f32[16,1024]{1,0:T(8,128)} %bitcast.9, f32[8,128]{1,0:T(8,128)} %bitcast.10, ...), custom_call_target="tpu_custom_call" | custom-call | tf_op jit(solution)/shard_map/pallas_call | solution.py:603
  96.2 1.9 %copy.14 = bf16[256,1024]{1,0:T(8,128)(2,1)} copy(bf16[256,1024]{1,0:T(8,128)(2,1)} %get-tuple-element.8) | data formatting | bytes 1048576
  98.1 1.2 %copy.15 = f32[256]{0:T(256)} copy(f32[256]{0:T(256)} %bitcast.13) | data formatting | bytes 2048

commit v2 on v1

--- a/solution.py
+++ b/solution.py
@@ -24,16 +24,22 @@
     Y,
     x_hbm,
     res_hbm,
+    taps_hbm,
+    rates_hbm,
+    resid_hbm,
+    skip_hbm,
+    w_hbm,
+    gain_hbm,
+    emb_hbm,
+    ids_hbm,
+    bo_hbm,
+    ll_ref,
     taps_ref,
     rates_ref,
     resid_ref,
     skip_ref,
-    w_hbm,
     gain_ref,
-    emb_hbm,
     ids_ref,
-    bo_hbm,
-    ll_ref,
     x_v,
     xf,
     taps,
@@ -55,6 +61,7 @@
     w_all,
     a_all,
     c_send,
+    c_relay,
     c_recv,
     o_send,
     o_recv,
@@ -80,6 +87,8 @@
     a_rsem,
     c_ssem,
     c_rsem,
+    r_ssem,
+    r_rsem,
     o_ssem,
     o_rsem,
     l_sem,
@@ -88,7 +97,7 @@
     T = x_hbm.shape[1]
     C = x_hbm.shape[2]
     LN = C // SUB
-    modes = rates_ref.shape[0]
+    modes = rates_hbm.shape[0]
     MQ = modes // GROUP
     QR = MQ * SUB
     KH = w_hbm.shape[0] // 2
@@ -98,6 +107,7 @@
     NX = 4
     VB = emb_hbm.shape[0] // CHAN
     HT = T // 2
+    QS = T // Y // 2
 
     seq = lax.axis_index("seq")
     chan = lax.axis_index("chan")
@@ -115,6 +125,10 @@
     def x_dev(xn):
         return dev(z, (xn // 2) * 2 + core, (xn % 2) * Y + y)
 
+    def chip_dev(n):
+        xn, yn = n // Y, n % Y
+        return dev(z, (xn // 2) * 2 + core, (xn % 2) * Y + yn)
+
     def rcopy(src, dst, ssem, rsem, target):
         return pltpu.make_async_remote_copy(
             src_ref=src, dst_ref=dst, send_sem=ssem, recv_sem=rsem, device_id=target, device_id_type=MESH
@@ -124,8 +138,8 @@
     partners = [dev((z + d) % Z, g, chan) for d in range(1, Z)]
     partners += [dev(z, (g + r) % 4, chan) for r in range(1, 4)]
     partners += [{"seq": (seq + 1) % SEQ, "chan": chan}, {"seq": (seq + SEQ - 1) % SEQ, "chan": chan}]
-    partners += [x_dev((xx + r) % NX) for r in range(1, NX)]
-    partners += [dev(z, g, (chan + r) % CHAN) for r in range(1, CHAN)]
+    here = xx * Y + y
+    partners += [chip_dev((here + r) % (NX * Y)) for r in range(1, NX * Y)]
     swap = dev(z, x_hi * 2 + (1 - core), (1 - x_lo) * Y + y)
     partners += [swap]
     for partner in partners:
@@ -135,17 +149,32 @@
     load_res = pltpu.make_async_copy(res_hbm, res_v, loc_sem.at[3])
     load_emb = pltpu.make_async_copy(emb_hbm, emb_v, loc_sem.at[4])
     load_w = pltpu.make_async_copy(w_hbm, w_all.at[core, z], loc_sem.at[5])
+    smalls = [
+        pltpu.make_async_copy(src, dst, loc_sem.at[7 + n])
+        for n, (src, dst) in enumerate(
+            (
+                (rates_hbm, rates_ref),
+                (resid_hbm, resid_ref),
+                (taps_hbm, taps_ref),
+                (skip_hbm, skip_ref),
+                (gain_hbm, gain_ref),
+                (ids_hbm, ids_ref),
+            )
+        )
+    ]
     native = core == x_lo
 
     @pl.when(native)
     def _():
         load_w.start()
 
-    for load in loads:
+    for load in smalls + loads:
         load.start()
     load_res.start()
     load_emb.start()
 
+    for load in smalls:
+        load.wait()
     for j in range(SUB):
         lanes = slice(j * LN, (j + 1) * LN)
         rate[pl.ds(j, modes, stride=SUB), :] = rates_ref[:, lanes]
@@ -167,20 +196,67 @@
                 block = x_v[i, rows, j * LN : (j + 1) * LN].astype(F32)
                 xf[i, pl.ds(b * PAIR * SUB + j, PAIR, stride=SUB), :] = block
 
-    spread(T // PAIR - 1)
+    lax.fori_loop(0, T // PAIR, lambda b, c: (spread(b), c)[1], 0)
+
+    def tap(t, i):
+        return taps[(t * STREAMS + i) * SUB : (t * STREAMS + i + 1) * SUB, :]
+
+    def rows_of(t):
+        return pl.ds(pl.multiple_of(t * SUB, SUB), SUB)
+
+    def short(i, now, before, before2):
+        return tap(0, i) * now + tap(1, i) * before + tap(2, i) * before2
+
+    def mode(ref, m):
+        return ref[m * SUB : (m + 1) * SUB, :]
+
+    UN = 4
+    zero = jnp.zeros((SUB, LN), F32)
+
+    def state_one(rows, carry):
+        k1, k2, v1, v2, *s = carry
+        k0, v0 = xf[1, rows, :], xf[2, rows, :]
+        value = short(1, k0, k1, k2) * short(2, v0, v1, v2)
+        kv[rows, :] = value
+        s = [mode(dec1, m) * s[m] + value for m in range(modes)]
+        return (k0, k1, v0, v1, *s)
+
+    def state_step(n, carry):
+        for u in range(UN):
+            carry = state_one(rows_of(n * UN + u), carry)
+        return carry
+
+    def at(i, t):
+        return xf[i, t * SUB : (t + 1) * SUB, :]
+
+    last = (at(1, 1), at(1, 0), at(2, 1), at(2, 0)) + (zero,) * modes
+    for t in range(HALO, UN):
+        last = state_one(rows_of(t), last)
+    last = lax.fori_loop(
+        1,
+        T // UN,
+        state_step,
+        last,
+    )
+    for m in range(modes):
+        st[m * SUB : (m + 1) * SUB, :] = last[4 + m]
+    dec_a = jnp.exp(-rate[...] * float(T - 2))
+
     pl.semaphore_wait(barrier, len(partners))
 
-    halo_copy = rcopy(
+    def halo_(): return rcopy(
         xf.at[:, pl.ds((T - HALO) * SUB, HALO * SUB), :],
         halo,
         halo_sem.at[0],
         halo_sem.at[1],
         {"seq": (seq + 1) % SEQ, "chan": chan},
     )
+    halo_copy = halo_()
     halo_copy.start()
 
-    swap_copy = rcopy(w_hbm, w_all.at[x_lo, z], sw_sem.at[0], sw_sem.at[1], swap)
-
+    def swap_(): return rcopy(w_hbm, w_all.at[x_lo, z], sw_sem.at[0], sw_sem.at[1], swap)
+
+    swap_copy = swap_()
     @pl.when(jnp.logical_not(native))
     def _():
         swap_copy.start()
@@ -214,75 +290,65 @@
         ref = w_chunk(core, rel(i), h)
         return rcopy(ref, ref, sib_ssem.at[i, h], sib_rsem.at[i, h], sibling)
 
+    def ring_first():
+        for flow in range(2):
+            ring_copy(flow, 1, 0).start()
+        for h in range(2):
+            sib_copy(0, h).start()
+
+    def ring_second():
+        for flow in range(2):
+            ring_copy(flow, 1, 0).wait_send()
+        for flow in range(2):
+            ring_copy(flow, 1, 1).start()
+
     @pl.when(native)
     def _():
         load_w.wait()
-
-    @pl.when(jnp.logical_not(native))
-    def _():
-        rcopy(w_hbm, w_all.at[core, z], sw_sem.at[0], sw_sem.at[1], swap).wait_recv()
-
-    for h in range(2):
+        ring_first()
+        ring_second()
+
+    def pump(d, h):
         for flow in range(2):
-            if HALF == 1 and h not in ring_halves(flow, 1):
+            if h not in ring_halves(flow, d):
                 continue
-            ring_copy(flow, 1, h).start()
-    for h in range(2):
-        sib_copy(0, h).start()
-
-    def pump(d):
-        for h in range(2):
-            for flow in range(2):
-                if h not in ring_halves(flow, d):
-                    continue
-                ring_copy(flow, d, h).wait_recv()
-                if d < HALF and h in ring_halves(flow, d + 1):
-                    ring_copy(flow, d + 1, h).start()
-                i = Z - 1 if d == HALF else (2 * d if flow == 0 else 2 * d - 1)
-                sib_copy(i, h).start()
-
-    lax.fori_loop(0, T // PAIR - 1, lambda b, c: (spread(b), c)[1], 0)
+            ring_copy(flow, d, h).wait_recv()
+            if d < HALF and h in ring_halves(flow, d + 1):
+                ring_copy(flow, d + 1, h).start()
+            i = Z - 1 if d == HALF else (2 * d if flow == 0 else 2 * d - 1)
+            sib_copy(i, h).start()
+
+    def other_start():
+        @pl.when(jnp.logical_not(native))
+        def _():
+            swap_().wait_recv()
+            ring_first()
+
+    def pumps(cond, *steps):
+        @pl.when(cond)
+        def _():
+            for d, h in steps:
+                pump(d, h)
+
+    other = jnp.logical_not(native)
 
     halo_copy.wait_recv()
     first = seq == 0
 
-    def tap(t, i):
-        return taps[(t * STREAMS + i) * SUB : (t * STREAMS + i + 1) * SUB, :]
-
     def halo_tile(i, n):
         return jnp.where(first, 0.0, halo[i, n * SUB : (n + 1) * SUB, :])
 
-    def rows_of(t):
-        return pl.ds(pl.multiple_of(t * SUB, SUB), SUB)
-
-    def short(i, now, before, before2):
-        return tap(0, i) * now + tap(1, i) * before + tap(2, i) * before2
-
-    def mode(ref, m):
-        return ref[m * SUB : (m + 1) * SUB, :]
-
-    UN = 4
-    zero = jnp.zeros((SUB, LN), F32)
-
-    def state_step(n, carry):
-        k1, k2, v1, v2, *s = carry
-        for u in range(UN):
-            rows = rows_of(n * UN + u)
-            k0, v0 = xf[1, rows, :], xf[2, rows, :]
-            value = short(1, k0, k1, k2) * short(2, v0, v1, v2)
-            kv[rows, :] = value
-            s = [mode(dec1, m) * s[m] + value for m in range(modes)]
-            k1, k2, v1, v2 = k0, k1, v0, v1
-        return (k1, k2, v1, v2, *s)
-
-    last = lax.fori_loop(
-        0,
-        T // UN,
-        state_step,
-        (halo_tile(1, 1), halo_tile(1, 0), halo_tile(2, 1), halo_tile(2, 0)) + (zero,) * modes,
-    )
+    heads = []
+    for t in range(HALO):
+        pair = []
+        for i in (1, 2):
+            seen = [halo_tile(i, 0), halo_tile(i, 1), at(i, 0), at(i, 1)]
+            pair.append(short(i, seen[t + 2], seen[t + 1], seen[t]))
+        heads.append(pair[0] * pair[1])
+        kv[t * SUB : (t + 1) * SUB, :] = heads[t]
     for m in range(modes):
-        st[m * SUB : (m + 1) * SUB, :] = last[4 + m]
+        rows = slice(m * SUB, (m + 1) * SUB)
+        st[rows, :] += dec_a[rows, :] * (mode(dec1, m) * heads[0] + heads[1])
 
     def quarter(j):
         return pl.ds(pl.multiple_of(j * QR, QR), QR)
@@ -309,6 +375,8 @@
             q1, q2 = q0, q1
         return (q1, q2, *s)
 
+    pumps(native, (1, 0))
+    half_way = lax.fori_loop(0, T // UN // 2, local_step, (halo_tile(0, 1), halo_tile(0, 0)) + (zero,) * modes)
     for r in range(1, 4):
         p1_copy(r).wait_recv()
     my_t = dec_t[quarter(g), :]
@@ -322,7 +390,10 @@
 
     lax.fori_loop(z + 1, Z, lambda zz, c: (p2_copy(zz, z).start(), c)[1], 0)
 
-    lax.fori_loop(0, T // UN, local_step, (halo_tile(0, 1), halo_tile(0, 0)) + (zero,) * modes)
+    other_start()
+    pumps(native, (1, 1))
+    lax.fori_loop(T // UN // 2, T // UN, local_step, half_way)
+    pumps(native, (2, 0))
 
     my_g = dec_g[quarter(g), :]
 
@@ -342,7 +413,13 @@
     for r in range(1, 4):
         p3_copy(r).start()
     p3[quarter(g), :] = p3_send[g]
-    pump(1)
+
+    @pl.when(other)
+    def _():
+        ring_second()
+
+    pumps(native, (2, 1))
+    pumps(other, (1, 0))
     for r in range(1, 4):
         p3_copy(r).wait_recv()
 
@@ -370,117 +447,197 @@
 
     right, left = (xx + 1) % NX, (xx + NX - 1) % NX
 
-    def a_copy(way, block, h, slot):
-        ref = a_all.at[block, pl.ds(h * HT, HT), :]
-        return rcopy(ref, ref, a_ssem.at[slot, h], a_rsem.at[slot, h], x_dev(right if way == 0 else left))
-
-    for h in range(2):
-        a_copy(0, xx, h, 0).start()
-        a_copy(1, xx, 1 - h, 1).start()
-
-    pump(2)
-    a_copy(0, left, 0, 0).wait_recv()
-    a_copy(0, left, 0, 2).start()
-    a_copy(1, right, 1, 1).wait_recv()
-    a_copy(1, right, 1, 2).start()
-    a_copy(0, left, 1, 0).wait_recv()
-    a_copy(1, right, 0, 1).wait_recv()
-
-    def c_copy(tb, zz):
-        peer, half = zz % Y, zz // Y
-        dy = (peer + Y - y) % Y
+    def a_copy(way, h, relay):
+        rows = pl.ds(h * HT + (way * HT // 2 if relay else 0), HT // 2 if relay else HT)
+        return rows, way + 2 * relay, x_dev(right if way == 0 else left)
+
+    def a_out(way, h, relay=0):
+        rows, slot, target = a_copy(way, h, relay)
+        ref = a_all.at[(left if way == 0 else right) if relay else xx, rows, :]
+        return rcopy(ref, ref, a_ssem.at[slot, h], a_rsem.at[slot, h], target)
+
+    def a_in(way, h, relay=0):
+        rows, slot, target = a_copy(way, h, relay)
+        ref = a_all.at[(xx + 2) % NX if relay else (left if way == 0 else right), rows, :]
+        return rcopy(ref, ref, a_ssem.at[slot, h], a_rsem.at[slot, h], target)
+
+    def a_pass(h):
+        for way in range(2):
+            a_in(way, h).wait_recv()
+            a_out(way, h, 1).start()
+
+    def a_far(h):
+        for way in range(2):
+            a_in(way, h, 1).wait_recv()
+
+    for way in range(2):
+        a_out(way, 0).start()
+    pumps(native, (3, 0))
+    pumps(other, (1, 1))
+    for way in range(2):
+        a_out(way, 0).wait_send()
+        a_out(way, 1).start()
+    pumps(native, (3, 1))
+    pumps(other, (2, 0))
+
+    GROUPS = ((0, 3), (3, 5), (5, 7), (7, 8))
+
+    def span(n):
+        return pl.ds(GROUPS[n][0], GROUPS[n][1] - GROUPS[n][0])
+
+    def y_next(way):
+        return (y + 1) % Y if way == 0 else (y + Y - 1) % Y
+
+    def r_copy(tb, n, way):
         return rcopy(
-            c_send.at[tb, zz],
-            c_recv.at[jnp.maximum(dy - 1, 0), tb, half],
-            c_ssem.at[tb, zz],
-            c_rsem.at[jnp.maximum(dy - 1, 0), tb, half],
-            dev(z, g, x_lo * Y + peer),
+            c_send.at[tb, (y + 2) % Y, span(n), way],
+            c_relay.at[way, tb, span(n)],
+            r_ssem.at[way, tb, n],
+            r_rsem.at[way, tb, n],
+            dev(z, g, x_lo * Y + y_next(way)),
         )
 
-    def unit(tb, i):
-        zz = rel(i)
-        total = jnp.dot(a_all[2 * tb], w_all[0, zz], preferred_element_type=F32)
-        total += jnp.dot(a_all[2 * tb + 1], w_all[1, zz], preferred_element_type=F32)
-        c_send[tb, zz] = total.astype(BF16)
-
-        @pl.when(zz % Y != y)
-        def _():
-            c_copy(tb, zz).start()
+    def c_copy(tb, n, way):
+        return rcopy(
+            c_send.at[tb, y_next(way), span(n)],
+            c_recv.at[way, tb, span(n)],
+            c_ssem.at[way, tb, n],
+            c_rsem.at[way, tb, n],
+            dev(z, g, x_lo * Y + y_next(way)),
+        )
+
+    def relay(tb, n):
+        for way in range(2):
+            r_copy(tb, n, way).wait_recv()
+            peer = y_next(way)
+
+            def step(i, c):
+                mine = c_send[tb, peer, i, way].astype(F32)
+                c_send[tb, peer, i, way] = (mine + c_relay[way, tb, i].astype(F32)).astype(BF16)
+                return c
+
+            lax.fori_loop(GROUPS[n][0], GROUPS[n][1], step, 0)
+            c_copy(tb, n, way).start()
 
     def sib_wait(i):
         for h in range(2):
             ref = w_chunk(1 - core, rel(i), h)
             rcopy(ref, ref, sib_ssem.at[i, h], sib_rsem.at[i, h], sibling).wait_recv()
 
-    NEAR = max(Z - 3, 1)
-
-    def near_first(i, c):
-        sib_wait(i)
-        unit(x_hi, i)
-        return c
-
-    def near_second(i, c):
-        unit(1 - x_hi, i)
-        return c
-
-    def both(i, c):
-        sib_wait(i)
-        unit(x_hi, i)
-        unit(1 - x_hi, i)
-        return c
-
-    lax.fori_loop(0, NEAR, near_first, 0)
-    for d in range(3, HALF):
-        pump(d)
-    a_copy(0, (xx + 2) % NX, 0, 2).wait_recv()
-    a_copy(1, (xx + 2) % NX, 1, 2).wait_recv()
-    lax.fori_loop(0, NEAR, near_second, 0)
-    lax.fori_loop(NEAR, Z - 1, both, 0)
-    if HALF > 2:
-        pump(HALF)
-    lax.fori_loop(Z - 1, Z, both, 0)
-
-    def o_copy(tb, half):
-        target = 2 * tb + half
-        r = (target + NX - xx) % NX
+    def unit(tb, i, halves):
+        zz = rel(i)
+        rows = pl.ds(halves[0] * HT, len(halves) * HT)
+        total = jnp.dot(a_all[2 * tb, rows, :], w_all[0, zz], preferred_element_type=F32)
+        total += jnp.dot(a_all[2 * tb + 1, rows, :], w_all[1, zz], preferred_element_type=F32)
+        value = total.astype(BF16)
+        for at_, h in enumerate(halves):
+            for n in range(Y):
+                c_send[tb, n, i, h] = value[at_ * HT + n * QS : at_ * HT + (n + 1) * QS, :]
+
+    def units(tb, n, halves, fresh=False):
+        def step(i, c):
+            if fresh:
+                sib_wait(i)
+            unit(tb, i, halves)
+            return c
+
+        lax.fori_loop(GROUPS[n][0], GROUPS[n][1], step, 0)
+        for way in range(2):
+            r_copy(tb, n, way).start()
+
+    def o_copy(tb, i):
+        zz = rel(i)
         return rcopy(
-            o_send.at[tb, half], o_recv.at[xx], o_ssem.at[tb, half], o_rsem.at[jnp.maximum(r - 1, 0)], x_dev(target)
+            o_send.at[tb, i],
+            o_recv.at[xx, :, y],
+            o_ssem.at[tb, i],
+            o_rsem.at[here],
+            dev(z, tb * 2 + core, zz),
         )
 
-    def sum_step(n, c):
-        tb = (x_hi + n // 2) % 2
-        half = n % 2
-        total = c_send[tb, half * Y + y].astype(F32)
-        for dy in range(1, Y):
-            src = c_recv.at[dy - 1, tb, half]
-            rcopy(src, src, c_ssem.at[tb, half], c_rsem.at[dy - 1, tb, half], sibling).wait_recv()
-            total += c_recv[dy - 1, tb, half].astype(F32)
-        value = total.astype(BF16)
-        mine = 2 * tb + half == xx
-
-        @pl.when(mine)
-        def _():
-            o_recv[xx] = value
-
-        @pl.when(jnp.logical_not(mine))
-        def _():
-            o_send[tb, half] = value
-            o_copy(tb, half).start()
-
-        return c
-
-    lax.fori_loop(0, 4, sum_step, 0)
+    def is_mine(tb, i):
+        return jnp.logical_and(tb == x_hi, rel(i) == chan)
+
+    def sum_group(tb, n):
+        for way in range(2):
+            c_copy(tb, n, way).wait_recv()
+
+        def step(i, c):
+            total = c_send[tb, y, i].astype(F32)
+            for way in range(2):
+                total += c_recv[way, tb, i].astype(F32)
+            value = total.astype(BF16)
+
+            @pl.when(is_mine(tb, i))
+            def _():
+                o_recv[xx, :, y] = value
+
+            @pl.when(jnp.logical_not(is_mine(tb, i)))
+            def _():
+                o_send[tb, i] = value
+                o_copy(tb, i).start()
+
+            return c
+
+        lax.fori_loop(GROUPS[n][0], GROUPS[n][1], step, 0)
+
+    near, far = x_hi, 1 - x_hi
+    whole = (0, 1)
+    a_pass(0)
+    pumps(other, (2, 1))
+    a_pass(1)
+    units(near, 0, whole, True)
+    pumps(other, (3, 0))
+    units(near, 1, whole, True)
+    pumps(other, (3, 1))
+    relay(near, 0)
+    pumps(native, (4, 0), (4, 1))
+    a_far(0)
+    a_far(1)
+    units(far, 0, whole)
+    relay(near, 1)
+    units(far, 1, whole)
+    units(near, 2, whole, True)
+    relay(far, 0)
+    units(far, 2, whole)
+    relay(far, 1)
+    relay(near, 2)
+    relay(far, 2)
+    pumps(other, (4, 0), (4, 1))
+    units(near, 3, whole, True)
+    units(far, 3, whole)
+
+    sum_group(near, 0)
+    sum_group(near, 1)
+    relay(near, 3)
+    relay(far, 3)
+    sum_group(far, 0)
+    sum_group(far, 1)
+    sum_group(near, 2)
+    sum_group(far, 2)
+    sum_group(near, 3)
+    sum_group(far, 3)
     load_res.wait()
     load_emb.wait()
-    for r in range(1, NX):
-        src = o_recv.at[(xx + NX - r) % NX]
-        rcopy(src, src, o_ssem.at[0, 0], o_rsem.at[r - 1], sibling).wait_recv()
+
+    def o_in(n):
+        ref = o_recv.at[n // Y, :, n % Y]
+        return rcopy(ref, ref, o_ssem.at[0, 0], o_rsem.at[n], sibling)
+
+    def o_wait(n, c):
+        @pl.when(n != here)
+        def _():
+            o_in(n).wait_recv()
+
+        return c
+
+    lax.fori_loop(0, NX * Y, o_wait, 0)
 
     squares = jnp.zeros((T, LN), F32)
     scaled = []
     for j in range(NX):
         cols = slice(j * NB, (j + 1) * NB)
-        value = (res_v[:, cols].astype(F32) + o_recv[j].astype(F32)).astype(BF16)
+        value = (res_v[:, cols].astype(F32) + o_recv[j].reshape(T, NB).astype(F32)).astype(BF16)
         bo_v[:, cols] = value
         wide = value.astype(F32)
         for n in range(NB // LN):
@@ -550,7 +707,8 @@
     for flow in range(2):
         for d in range(1, HALF + 1):
             for h in ring_halves(flow, d):
-                ring_copy(flow, d, h).wait_send()
+                if (d, h) != (1, 0):
+                    ring_copy(flow, d, h).wait_send()
     for i in range(Z):
         for h in range(2):
             sib_copy(i, h).wait_send()
@@ -558,31 +716,26 @@
         p1_copy(r).wait_send()
         p3_copy(r).wait_send()
     lax.fori_loop(z + 1, Z, lambda zz, c: (p2_copy(zz, z).wait_send(), c)[1], 0)
-    for h in range(2):
-        a_copy(0, xx, h, 0).wait_send()
-        a_copy(1, xx, h, 1).wait_send()
-    a_copy(0, left, 0, 2).wait_send()
-    a_copy(1, right, 1, 2).wait_send()
-
-    def c_done(n, c):
-        tb, zz = n // Z, n % Z
-
-        @pl.when(zz % Y != y)
+    for way in range(2):
+        a_out(way, 1).wait_send()
+        for h in range(2):
+            a_out(way, h, 1).wait_send()
+    for tb in range(2):
+        for n in range(len(GROUPS)):
+            for way in range(2):
+                r_copy(tb, n, way).wait_send()
+                c_copy(tb, n, way).wait_send()
+
+    def o_done(n, c):
+        tb, i = n // Z, n % Z
+
+        @pl.when(jnp.logical_not(is_mine(tb, i)))
         def _():
-            c_copy(tb, zz).wait_send()
+            o_copy(tb, i).wait_send()
 
         return c
 
-    lax.fori_loop(0, 2 * Z, c_done, 0)
-
-    def o_done(n, c):
-        @pl.when(n != xx)
-        def _():
-            o_copy(n // 2, n % 2).wait_send()
-
-        return c
-
-    lax.fori_loop(0, 4, o_done, 0)
+    lax.fori_loop(0, 2 * Z, o_done, 0)
     for r in range(1, CHAN):
         l_copy(r).wait_send()
         s_copy(r).wait_send()
@@ -597,15 +750,22 @@
     V = embedding.shape[0]
     CHAN = 2 * Y
     VB = V // CHAN
+    QS = T // Y // 2
     DMA = pltpu.SemaphoreType.DMA
     hbm = pl.BlockSpec(memory_space=pl.ANY)
     vmem = pl.BlockSpec(memory_space=pltpu.VMEM)
     block_out, log_like = pl.pallas_call(
         functools.partial(kernel, Z, Y),
         out_shape=(jax.ShapeDtypeStruct((T, C), BF16), jax.ShapeDtypeStruct((1, T), F32)),
-        in_specs=[hbm, hbm, vmem, vmem, vmem, vmem, hbm, vmem, hbm, vmem],
+        in_specs=[hbm] * 10,
         out_specs=(hbm, vmem),
         scratch_shapes=[
+            pltpu.VMEM((TAPS, STREAMS, C), F32),
+            pltpu.VMEM((modes, C), F32),
+            pltpu.VMEM((modes, C), F32),
+            pltpu.VMEM((SUB, LN), F32),
+            pltpu.VMEM((1, C), F32),
+            pltpu.VMEM((1, T), jnp.int32),
             pltpu.VMEM((STREAMS, T, C), BF16),
             pltpu.VMEM((STREAMS, T * SUB, LN), F32),
             pltpu.VMEM((TAPS * STREAMS * SUB, LN), F32),
@@ -626,10 +786,11 @@
             pltpu.VMEM((modes * SUB, LN), F32),
             pltpu.VMEM((2, Z, K, NB), BF16),
             pltpu.VMEM((4, T, C), BF16),
-            pltpu.VMEM((2, Z, T, NB), BF16),
-            pltpu.VMEM((Y - 1, 2, 2, T, NB), BF16),
-            pltpu.VMEM((2, 2, T, NB), BF16),
-            pltpu.VMEM((4, T, NB), BF16),
+            pltpu.VMEM((2, Y, Z, 2, QS, NB), BF16),
+            pltpu.VMEM((2, 2, Z, QS, NB), BF16),
+            pltpu.VMEM((2, 2, Z, 2, QS, NB), BF16),
+            pltpu.VMEM((2, Z, 2, QS, NB), BF16),
+            pltpu.VMEM((4, 2, Y, QS, NB), BF16),
             pltpu.VMEM((T, C), BF16),
             pltpu.VMEM((V, C), BF16),
             pltpu.VMEM((T, C), BF16),
@@ -637,7 +798,7 @@
             pltpu.VMEM((CHAN - 1, VB + PAIR, T), BF16),
             pltpu.VMEM((SUB, T), F32),
             pltpu.VMEM((CHAN - 1, SUB, T), F32),
-            DMA((7,)),
+            DMA((13,)),
             DMA((2,)),
             DMA((2, 3)),
             DMA((Z,)),
@@ -648,12 +809,14 @@
             DMA((Z, 2)),
             DMA((Z, 2)),
             DMA((Z, 2)),
-            DMA((3, 2)),
-            DMA((3, 2)),
+            DMA((4, 2)),
+            DMA((4, 2)),
+            DMA((2, 2, 4)),
+            DMA((2, 2, 4)),
+            DMA((2, 2, 4)),
+            DMA((2, 2, 4)),
             DMA((2, Z)),
-            DMA((Y - 1, 2, 2)),
-            DMA((2, 2)),
-            DMA((3,)),
+            DMA((4 * Y,)),
             DMA((2, CHAN - 1)),
             DMA((2, CHAN - 1)),
         ],

time: 99.5 us -> 98.5 us (0.990)
  Pallas kernels: 95.6 us -> 94.6 us
where the time goes in v2:
time: 98.5 us; the launch traced here: 98.3 us
  Pallas kernels  94.6 us (96%)
  local copies, waits for them, and re-layouts  3.07 us (3%)
    pallas_call x1, Pallas kernels, block(): pl.pallas_call(functools.partial(kernel, Z, Y), out_shape=(jax.ShapeDtype...  94.6 us
    unnamed x2, local copies, waits for them, and re-layouts  3.07 us

profile of v2, /device:TPU:6, one launch (start us, length us, event | category | flops | bytes accessed | tf_op | source)
XLA Modules:
  0.0 98.3 jit_solution(6107858943091486329)
XLA Ops:
  0.6 94.6 %shard_map.113 = (bf16[256,1024]{1,0:T(8,128)(2,1)}, f32[1,256]{1,0:T(1,128)}) custom-call(bf16[3,256,1024]{2,1,0:T(8,128)(2,1)} %bitcast.7, bf16[256,1024]{1,0:T(8,128)(2,1)} %res_hbm.1, f32[3,3,1024]{2,1,0:T(4,128)} %taps_hbm.1, f32[16,1024]{1,0:T(8,128)} %bitcast.8, f32[16,1024]{1,0:T(8,128)} %bitcast.9, f32[8,128]{1,0:T(8,128)} %bitcast.10, ...), custom_call_target="tpu_custom_call" | custom-call | tf_op jit(solution)/shard_map/pallas_call | solution.py:757
  95.3 1.9 %copy.14 = bf16[256,1024]{1,0:T(8,128)(2,1)} copy(bf16[256,1024]{1,0:T(8,128)(2,1)} %get-tuple-element.8) | data formatting | bytes 1048576
  97.1 1.2 %copy.15 = f32[256]{0:T(256)} copy(f32[256]{0:T(256)} %bitcast.13) | data formatting | bytes 2048

commit v3 on v2

--- a/solution.py
+++ b/solution.py
@@ -631,11 +631,11 @@
 
         return c
 
-    lax.fori_loop(0, NX * Y, o_wait, 0)
 
     squares = jnp.zeros((T, LN), F32)
-    scaled = []
+    logits = jnp.zeros((VB * CHAN, T), F32)
     for j in range(NX):
+        lax.fori_loop(j * Y, (j + 1) * Y, o_wait, 0)
         cols = slice(j * NB, (j + 1) * NB)
         value = (res_v[:, cols].astype(F32) + o_recv[j].reshape(T, NB).astype(F32)).astype(BF16)
         bo_v[:, cols] = value
@@ -643,15 +643,11 @@
         for n in range(NB // LN):
             part = wide[:, n * LN : (n + 1) * LN]
             squares += part * part
-        scaled.append((wide * gain_ref[:, cols]).astype(BF16))
+        scaled = (wide * gain_ref[:, cols]).astype(BF16)
+        logits += lax.dot_general(emb_v[:, cols], scaled, (((1,), (1,)), ((), ())), preferred_element_type=F32)
     store_bo = pltpu.make_async_copy(bo_v, bo_hbm, loc_sem.at[6])
     store_bo.start()
 
-    logits = jnp.zeros((VB * CHAN, T), F32)
-    for j in range(NX):
-        logits += lax.dot_general(
-            emb_v[:, j * NB : (j + 1) * NB], scaled[j], (((1,), (1,)), ((), ())), preferred_element_type=F32
-        )
     sums = jnp.sum(squares.T, axis=0, keepdims=True)
     high = sums.astype(BF16)
     low = (sums - high.astype(F32)).astype(BF16)

time: 98.5 us -> 99.3 us (level)
  no operation moved by 1% of the time
where the time goes in v3:
time: 99.3 us; the launch traced here: 99.2 us
  Pallas kernels  95.5 us (96%)
  local copies, waits for them, and re-layouts  3.07 us (3%)
    pallas_call x1, Pallas kernels, block(): pl.pallas_call(functools.partial(kernel, Z, Y), out_shape=(jax.ShapeDtype...  95.5 us
    unnamed x2, local copies, waits for them, and re-layouts  3.07 us

profile of v3, /device:TPU:6, one launch (start us, length us, event | category | flops | bytes accessed | tf_op | source)
XLA Modules:
  0.0 99.2 jit_solution(853901943645944745)
XLA Ops:
  0.6 95.5 %shard_map.113 = (bf16[256,1024]{1,0:T(8,128)(2,1)}, f32[1,256]{1,0:T(1,128)}) custom-call(bf16[3,256,1024]{2,1,0:T(8,128)(2,1)} %bitcast.7, bf16[256,1024]{1,0:T(8,128)(2,1)} %res_hbm.1, f32[3,3,1024]{2,1,0:T(4,128)} %taps_hbm.1, f32[16,1024]{1,0:T(8,128)} %bitcast.8, f32[16,1024]{1,0:T(8,128)} %bitcast.9, f32[8,128]{1,0:T(8,128)} %bitcast.10, ...), custom_call_target="tpu_custom_call" | custom-call | tf_op jit(solution)/shard_map/pallas_call | solution.py:753
  96.1 1.9 %copy.14 = bf16[256,1024]{1,0:T(8,128)(2,1)} copy(bf16[256,1024]{1,0:T(8,128)(2,1)} %get-tuple-element.8) | data formatting | bytes 1048576
  98.0 1.2 %copy.15 = f32[256]{0:T(256)} copy(f32[256]{0:T(256)} %bitcast.13) | data formatting | bytes 2048
